TPU v7x, 32 devices: a whole 2x2x4 slice. The times are simulated.
32 devices in a mesh: segment: 2 (over x), dev: 16 (over z, y, core).
Axes of the slice: x: 2, y: 2, z: 4, core: 2. Of those that a mesh axis runs over, the one named last changes fastest.
Arguments:
- queries: bfloat16 [32, 8192], P(('segment', 'dev')), may hold values from -64 to 64
- page_ids: int32 [32, 4, 32], P(('segment', 'dev')), may hold values from 0 to 255, as said below
- key_pages: bfloat16 [512, 64, 128], P(('segment', 'dev')), may hold values from -6 to 6
- value_pages: bfloat16 [512, 64, 128], P(('segment', 'dev')), may hold values from -6 to 6
- out_weight: bfloat16 [16384, 16384], P(('segment', 'dev')), may hold values from -0.1875 to 0.1875
Outputs:
- block_out: bfloat16 [32, 16384], P(('segment', 'dev'))
Inputs may be any that keep to these rules, and one draw needn't show every extreme that they name: `page_ids`: within the rows of one device (aligned blocks of 1 row), at most 16 of the entries name pages of one device (id // 16); in every section one such device, the same for all of its row blocks, is named exactly 16 times from each block. The 32 ids of one row and key head are distinct.
All inputs are finite; a program needn't handle non-finite values.
Results may differ from a plain program's by a relative error of at most 0.006.
Values may be sent and summed in bfloat16 or wider, within the bound.
A program may use at most 64 MiB of HBM per device.

v0:
```python
import math

import jax
import jax.numpy as jnp
from jax import lax
from jax.sharding import PartitionSpec as P


def from_behind(value, axis, steps):
    count = lax.axis_size(axis)
    pairs = [(source, (source + steps) % count) for source in range(count)]
    return lax.ppermute(value, axis, pairs)


def request_layout(page_ids, pool_size, devices, capacity):
    owner_ids = (page_ids // pool_size).reshape(-1)
    slot_ids = (page_ids % pool_size).reshape(-1)
    onehot = (owner_ids[:, None] == jnp.arange(devices, dtype=jnp.int32)[None, :]).astype(jnp.int32)
    before = jnp.cumsum(onehot, axis=0) - onehot
    rank_ids = jnp.sum(before * onehot, axis=1)
    target = owner_ids * capacity + rank_ids
    slot_table = jnp.zeros((devices * capacity,), jnp.int32).at[target].set(slot_ids)
    return (target, slot_table.reshape(devices, capacity))


def page_partials(query_part, key_part, value_part, score_scale):
    scores = (
        jnp.einsum("...gd,...td->...gt", query_part, key_part, preferred_element_type=jnp.float32)
        * score_scale
    )
    page_max = jnp.max(scores, axis=-1)
    weights = jnp.exp(scores - page_max[..., None]).astype(jnp.bfloat16)
    weight_sum = jnp.sum(weights.astype(jnp.float32), axis=-1)
    partial_value = jnp.einsum(
        "...gt,...td->...gd", weights, value_part, preferred_element_type=jnp.float32
    )
    return (partial_value, page_max, weight_sum)


def local(queries, page_ids, key_pages, value_pages, out_weight):
    devices = lax.axis_size("dev")
    row_count = queries.shape[0]
    kv_heads = page_ids.shape[1]
    chosen = page_ids.shape[2]
    pool_size = key_pages.shape[0]
    page_tokens = key_pages.shape[1]
    head_dim = key_pages.shape[2]
    group_size = queries.shape[1] // (kv_heads * head_dim)
    capacity = 2 * row_count * kv_heads * chosen // devices
    score_scale = 1.0 / math.sqrt(head_dim)
    target, slot_table = request_layout(page_ids, pool_size, devices, capacity)
    grouped = queries.reshape(row_count, kv_heads, 1, group_size, head_dim)
    per_request = jnp.broadcast_to(grouped, (row_count, kv_heads, chosen, group_size, head_dim))
    per_request = per_request.reshape(-1, group_size, head_dim)
    asked_slots = lax.all_to_all(slot_table, "dev", split_axis=0, concat_axis=0, tiled=True)
    fetched_keys, fetched_values = (
        lax.all_to_all(key_pages[asked_slots], "dev", split_axis=0, concat_axis=0, tiled=True),
        lax.all_to_all(value_pages[asked_slots], "dev", split_axis=0, concat_axis=0, tiled=True),
    )
    request_keys = fetched_keys.reshape(devices * capacity, page_tokens, head_dim)[target]
    request_values = fetched_values.reshape(devices * capacity, page_tokens, head_dim)[target]
    partial_value, page_max, weight_sum = page_partials(
        per_request, request_keys, request_values, score_scale
    )
    request_shape = (row_count, kv_heads, chosen, group_size)
    page_max = page_max.reshape(request_shape)
    weight_sum = weight_sum.reshape(request_shape)
    partial_value = partial_value.reshape(request_shape + (head_dim,))
    highest = jnp.max(page_max, axis=2, keepdims=True)
    factor = jnp.exp(page_max - highest)
    numerator = jnp.sum(factor[..., None] * partial_value, axis=2)
    denominator = jnp.sum(factor * weight_sum, axis=2)
    attended = (numerator / denominator[..., None]).astype(jnp.bfloat16)
    attended = attended.reshape(row_count, devices, -1)
    by_heads = lax.all_to_all(attended, "dev", split_axis=1, concat_axis=0, tiled=True)
    by_heads = by_heads.reshape(row_count * devices, -1)
    projected = lax.psum_scatter(
        jnp.dot(by_heads, out_weight, preferred_element_type=jnp.float32),
        "dev",
        scatter_dimension=0,
        tiled=True,
    ).astype(jnp.bfloat16)
    return from_behind(projected, "segment", 1)


def solution(mesh):
    placed = (
        P(("segment", "dev"), None),
        P(("segment", "dev"), None, None),
        P(("segment", "dev"), None, None),
        P(("segment", "dev"), None, None),
        P(("segment", "dev"), None),
    )
    return jax.shard_map(
        local, mesh=mesh, in_specs=placed, out_specs=P(("segment", "dev"), None), check_vma=False
    )
```

profile of v0, /device:TPU:0, one launch (start us, length us, event | category | flops | bytes accessed | tf_op | source)
XLA Modules:
  0.0 314.6 jit_solution(13684596513684943242)
XLA Ops:
  0.0 0.7 broadcast_multiply_fusion
  0.8 0.1 fusion.3
  0.9 0.2 reduce_window_sum.11
  1.1 0.2 select_reduce_fusion
  1.4 1.0 scatter_custom_fusion
  2.4 0.1 all_to_all.21
  2.5 13.6 %all_to_all.31 = s32[16,1,16]{2,1,0:T(1,128)S(1)} all-to-all(s32[16,1,16]{2,1,0:T(1,128)S(1)} %all_to_all.21), channel_id=1, replica_groups=mesh['segment'=2,'dev'=16] {'dev'}, dimensions={0} | all-to-all | bytes 2048 | tf_op jit(solution)/shard_map/all_to_all | solution.py:55
  16.2 3.1 gather_fusion
  19.3 4.7 %all-to-all-start.1 = ((bf16[16,16,64,128]{3,2,1,0:T(8,128)(2,1)}), bf16[16,16,64,128]{3,2,1,0:T(8,128)(2,1)}, u32[]{:S(2)}, u32[]{:S(2)}) async-start(bf16[16,16,64,128]{3,2,1,0:T(8,128)(2,1)} %bitcast.36), calls=%async_computation.1 | async-start | bytes 8388608 | tf_op jit(solution)/shard_map/all_to_all | solution.py:57
  24.0 3.1 gather_fusion.2
  27.0 74.5 %all-to-all-done.1 = bf16[16,16,64,128]{3,2,1,0:T(8,128)(2,1)} async-done(((bf16[16,16,64,128]{3,2,1,0:T(8,128)(2,1)}), bf16[16,16,64,128]{3,2,1,0:T(8,128)(2,1)}, u32[]{:S(2)}, u32[]{:S(2)}) %all-to-all-start.1) | async-done | bytes 4194336 | tf_op jit(solution)/shard_map/all_to_all | solution.py:57
  101.6 19.8 %all-to-all-start.2 = ((bf16[16,16,64,128]{3,2,1,0:T(8,128)(2,1)}), bf16[16,16,64,128]{3,2,1,0:T(8,128)(2,1)}, u32[]{:S(2)}, u32[]{:S(2)}) async-start(bf16[16,16,64,128]{3,2,1,0:T(8,128)(2,1)} %bitcast.35), calls=%async_computation.2 | async-start | bytes 8388608 | tf_op jit(solution)/shard_map/all_to_all | solution.py:58
  121.4 0.1 reduce.3
  121.5 3.1 gather_fusion.1
  124.7 1.3 fusion.11
  126.0 0.7 convert_reduce_fusion
  126.7 72.4 %all-to-all-done.2 = bf16[16,16,64,128]{3,2,1,0:T(8,128)(2,1)} async-done(((bf16[16,16,64,128]{3,2,1,0:T(8,128)(2,1)}), bf16[16,16,64,128]{3,2,1,0:T(8,128)(2,1)}, u32[]{:S(2)}, u32[]{:S(2)}) %all-to-all-start.2) | async-done | bytes 4194336 | tf_op jit(solution)/shard_map/all_to_all | solution.py:58
  199.0 3.2 %gather_fusion.3 = bf16[128,64,128]{2,1,0:T(8,128)(2,1)S(1)} fusion(bf16[256,64,128]{2,1,0:T(8,128)(2,1)} %bitcast.9, s32[1024]{0:T(1024)S(1)} %pad_clamp_fusion), kind=kCustom, calls=%fused_computation.3 | custom fusion | bytes 4194816 | tf_op jit(solution)/shard_map/gather | solution.py:61
  202.2 0.7 fusion.1
  203.0 0.3 multiply_reduce_fusion
  203.5 0.5 broadcast.135
  204.0 0.7 reduce.4
  204.7 0.6 reshape.239
  205.3 19.6 %all-to-all-start.3 = ((bf16[16,2,256]{2,1,0:T(2,128)(2,1)}), bf16[16,2,256]{2,1,0:T(2,128)(2,1)S(1)}, u32[]{:S(2)}, u32[]{:S(2)}) async-start(bf16[16,2,256]{2,1,0:T(2,128)(2,1)} %reshape.239), calls=%async_computation.3 | async-start | bytes 32768 | tf_op jit(solution)/shard_map/all_to_all | solution.py:75
  225.0 0.7 dynamic-slice
  225.7 5.8 %all-to-all-done.3 = bf16[16,2,256]{2,1,0:T(2,128)(2,1)S(1)} async-done(((bf16[16,2,256]{2,1,0:T(2,128)(2,1)}), bf16[16,2,256]{2,1,0:T(2,128)(2,1)S(1)}, u32[]{:S(2)}, u32[]{:S(2)}) %all-to-all-start.3) | async-done | bytes 16416 | tf_op jit(solution)/shard_map/all_to_all | solution.py:75
  231.5 8.1 %fusion.4 = f32[16,16384]{1,0:T(8,128)S(1)} fusion(bf16[512,16384]{1,0:T(8,128)(2,1)} %param.9, bf16[1,16,512]{2,0,1:T(2,128)(2,1)S(1)} %bitcast.42), kind=kOutput, calls=%fused_computation.21 | convolution fusion | flops 268435456 | bytes 17842176 | tf_op jit(solution)/shard_map/dot_general | solution.py:78
  239.6 69.3 %all-reduce.2 = bf16[16,16384]{1,0:T(8,128)(2,1)S(1)} all-reduce(f32[16,16384]{1,0:T(8,128)S(1)} %fusion.4), channel_id=2, replica_groups=mesh['segment'=2,'dev'=16] {'dev'}, use_global_device_ids=true, to_apply=%region_8.9.clone | all-reduce | flops 262144 | bytes 1572864
  308.9 0.8 dynamic-slice_convert_fusion
  309.7 1.6 collective-permute-start
  311.2 2.8 collective-permute-done
  314.0 0.6 copy.15
  (23 shorter events, 0.6 us)
Async XLA Ops:
  0.0 16.2 %copy-start = (bf16[16,64,128]{2,1,0:T(8,128)(2,1)S(1)}, bf16[16,64,128]{2,1,0:T(8,128)(2,1)}, u32[]{:S(2)}) copy-start(bf16[16,64,128]{2,1,0:T(8,128)(2,1)} %param.7) | copy-start | bytes 786436
  19.3 4.7 %copy-start.1 = (bf16[16,64,128]{2,1,0:T(8,128)(2,1)S(1)}, bf16[16,64,128]{2,1,0:T(8,128)(2,1)}, u32[]{:S(2)}) copy-start(bf16[16,64,128]{2,1,0:T(8,128)(2,1)} %param.8) | copy-start | bytes 786436
  19.3 82.3 %all-to-all-start.1 = ((bf16[16,16,64,128]{3,2,1,0:T(8,128)(2,1)}), bf16[16,16,64,128]{3,2,1,0:T(8,128)(2,1)}, u32[]{:S(2)}, u32[]{:S(2)}) async-start(bf16[16,16,64,128]{3,2,1,0:T(8,128)(2,1)} %bitcast.36), calls=%async_computation.1 | async-start | bytes 8388608 | tf_op jit(solution)/shard_map/all_to_all | solution.py:57
  101.6 19.8 %copy-start.2 = (bf16[1,8192]{1,0:T(2,128)(2,1)S(1)}, bf16[1,8192]{1,0:T(2,128)(2,1)}, u32[]{:S(2)}) copy-start(bf16[1,8192]{1,0:T(2,128)(2,1)} %param.5) | copy-start | bytes 49156
  101.6 97.5 %all-to-all-start.2 = ((bf16[16,16,64,128]{3,2,1,0:T(8,128)(2,1)}), bf16[16,16,64,128]{3,2,1,0:T(8,128)(2,1)}, u32[]{:S(2)}, u32[]{:S(2)}) async-start(bf16[16,16,64,128]{3,2,1,0:T(8,128)(2,1)} %bitcast.35), calls=%async_computation.2 | async-start | bytes 8388608 | tf_op jit(solution)/shard_map/all_to_all | solution.py:58
  199.0 25.9 %copy-start.3 = (u32[32]{0:T(128)S(1)}, u32[32]{0:T(128)}, u32[]{:S(2)}) copy-start(u32[32]{0:T(128)} %constant.52) | copy-start | bytes 388
  205.3 26.1 %all-to-all-start.3 = ((bf16[16,2,256]{2,1,0:T(2,128)(2,1)}), bf16[16,2,256]{2,1,0:T(2,128)(2,1)S(1)}, u32[]{:S(2)}, u32[]{:S(2)}) async-start(bf16[16,2,256]{2,1,0:T(2,128)(2,1)} %reshape.239), calls=%async_computation.3 | async-start | bytes 32768 | tf_op jit(solution)/shard_map/all_to_all | solution.py:75
  309.7 4.3 %collective-permute-start = (bf16[1,16384]{1,0:T(2,128)(2,1)S(1)}, bf16[1,16384]{1,0:T(2,128)(2,1)S(1)}, u32[]{:S(2)}, u32[]{:S(2)}) collective-permute-start(bf16[1,16384]{1,0:T(2,128)(2,1)S(1)} %dynamic-slice_convert_fusion), channel_id=1, source_target_pairs={{0,16},{16,0},{1,17},{17,1},{2,18},{18,2},{3,19},{19,3},{4,20},{20... | collective-permute-start | bytes 98312 | tf_op jit(solution)/shard_map/ppermute | solution.py:12
where the time goes:
time: 315 us
  waiting for transfers between devices  155 us (49%)
  blocking collectives  82.9 us (26%)
  starting transfers between devices  45.7 us (15%)
  local copies, waits for them, and re-layouts  17.1 us (5%)
  matrix products  10.1 us (3%)
  other arithmetic  3.19 us (1%)
    all_to_all x1, waiting for transfers between devices, local(): lax.all_to_all(key_pages[asked_slots], 'dev', split_axis=0, concat_axis=0...  74.5 us
    all_to_all x1, waiting for transfers between devices, local(): lax.all_to_all(value_pages[asked_slots], 'dev', split_axis=0, concat_axis...  72.4 us
    unnamed x1, blocking collectives  69.3 us
    all_to_all x1, starting transfers between devices, local(): lax.all_to_all(value_pages[asked_slots], 'dev', split_axis=0, concat_axis...  19.8 us
    all_to_all x1, starting transfers between devices, local(): lax.all_to_all(attended, 'dev', split_axis=1, concat_axis=0, tiled=True)  19.6 us
    all_to_all x1, blocking collectives, local(): lax.all_to_all(slot_table, 'dev', split_axis=0, concat_axis=0, tiled=True)  13.6 us
    dot_general x1, matrix products, local(): jnp.dot(by_heads, out_weight, preferred_element_type=jnp.float32)  8.06 us
  transfers between devices with their start and end apart: 4, of which 4 were waited for; matrix products, arithmetic and copies ran while one was open for 3% of the time, Pallas kernels for 0%

commit v1 on v0

v1 whole, which is shorter than its diff:
```python
import functools
import math

import jax
import jax.numpy as jnp
from jax import lax
from jax.experimental import pallas as pl
from jax.experimental.pallas import tpu as pltpu
from jax.sharding import PartitionSpec as P

MESH = pl.DeviceIdType.MESH
LANES = 128
CHUNKS = 4
BIG = float(2.0**100)


def kernel(dims, q_ref, ids_ref, key_ref, value_ref, weight_ref, out_ref,
           w_buf, k_buf, v_buf, page_hot, q_stage, q32, m_stage, q_buf, m_buf, q_aug, o_scr,
           p_send, p_recv, att, own_sum, c_send, c_recv, t_scr, f_send, f_recv,
           w_sem, kv_sem, kv_send, kv_recv, q_ssem, q_rsem, m_ssem, m_rsem, p_ssem, p_rsem,
           c_ssem, c_rsem, f_ssem, f_rsem):
    n, segments, kv_heads, chosen, pool, page, hd, group, width = dims
    half = n // 2
    hpd = kv_heads * group // n
    per_kv = group // 2
    tokens = pool * page
    span = 2 * pool
    cols = width // CHUNKS
    blocks = cols // LANES
    seg = lax.axis_index("segment")
    me = lax.axis_index("dev")
    core = lax.rem(me, 2)
    pair = me // 2
    mate = me + 1 - 2 * core
    slot = core * half + pair
    ahead = lax.rem(seg + 1, segments)
    behind = lax.rem(seg + segments - 1, segments)

    def weight_copy(k):
        return pltpu.make_async_copy(
            weight_ref.at[:, pl.ds(pl.multiple_of(k * cols, cols), cols)], w_buf.at[k], w_sem.at[k])

    barrier = pltpu.get_barrier_semaphore()

    @pl.loop(1, n)
    def _(k):
        pl.semaphore_signal(barrier, inc=1, device_id=(seg, lax.rem(me + k, n)), device_id_type=MESH)

    @pl.loop(0, half)
    def _(j):
        pl.semaphore_signal(barrier, inc=1, device_id=(behind, 2 * j + core), device_id_type=MESH)

    here = pl.ds(pl.multiple_of(core * tokens, tokens), tokens)
    key_local = pltpu.make_async_copy(key_ref, k_buf.at[here], kv_sem.at[0])
    value_local = pltpu.make_async_copy(value_ref, v_buf.at[here], kv_sem.at[1])
    key_local.start()
    value_local.start()

    @pl.loop(0, CHUNKS)
    def _(k):
        weight_copy(k).start()

    for c in range(2):
        for h in range(kv_heads):
            for u in range(per_kv // hpd):
                for i in range(hpd):
                    head = h * group + u * 2 * hpd + c * hpd + i
                    place = h * per_kv + u * hpd + i
                    q32[c, place:place + 1, :] = q_ref[0:1, head * hd:(head + 1) * hd].astype(jnp.float32)
    q_stage[...] = q32[...].astype(jnp.bfloat16)

    head_of_lane = lax.broadcasted_iota(jnp.int32, (kv_heads, LANES), 1) // span
    pick = (head_of_lane == lax.broadcasted_iota(jnp.int32, (kv_heads, LANES), 0)).astype(jnp.float32)
    ids = ids_ref[0].astype(jnp.float32)
    spread = lax.dot_general(ids, pick, (((0,), (0,)), ((), ())),
                             precision=lax.Precision.HIGHEST, preferred_element_type=jnp.float32)
    in_span = lax.rem(lax.broadcasted_iota(jnp.int32, (chosen, LANES), 1), span).astype(jnp.float32)
    offset = spread - in_span
    for j in range(half):
        hit = (jnp.abs(offset - float(j * span)) < 0.5).astype(jnp.float32)
        m_stage[j] = jnp.max(hit, axis=0, keepdims=True)

    q_buf[slot] = q_stage[core]
    m_buf[slot] = m_stage[pair]

    pl.semaphore_wait(barrier, n - 1 + half)

    def query_copy(k):
        peer = lax.rem(me + k, n)
        return pltpu.make_async_remote_copy(
            src_ref=q_stage.at[lax.rem(peer, 2)], dst_ref=q_buf.at[slot],
            send_sem=q_ssem.at[k], recv_sem=q_rsem.at[slot],
            device_id=(seg, peer), device_id_type=MESH)

    def mask_copy(k):
        peer = lax.rem(me + k, n)
        return pltpu.make_async_remote_copy(
            src_ref=m_stage.at[peer // 2], dst_ref=m_buf.at[slot],
            send_sem=m_ssem.at[k], recv_sem=m_rsem.at[slot],
            device_id=(seg, peer), device_id_type=MESH)

    @pl.loop(1, n)
    def _(k):
        query_copy(k).start()
        mask_copy(k).start()

    key_remote = pltpu.make_async_remote_copy(
        src_ref=key_ref, dst_ref=k_buf.at[here], send_sem=kv_send.at[0], recv_sem=kv_recv.at[0],
        device_id=(seg, mate), device_id_type=MESH)
    value_remote = pltpu.make_async_remote_copy(
        src_ref=value_ref, dst_ref=v_buf.at[here], send_sem=kv_send.at[1], recv_sem=kv_recv.at[1],
        device_id=(seg, mate), device_id_type=MESH)
    key_remote.start()
    value_remote.start()

    lane_page = lax.rem(lax.broadcasted_iota(jnp.int32, (2 * tokens, LANES), 1), span)
    token_page = lax.broadcasted_iota(jnp.int32, (2 * tokens, LANES), 0) // page
    page_hot[...] = jnp.where(lane_page == token_page, BIG, 0.0).astype(jnp.bfloat16)

    key_local.wait()
    value_local.wait()
    key_remote.wait()
    value_remote.wait()

    @pl.loop(1, n)
    def _(k):
        source = lax.rem(me + n - k, n)
        place = lax.rem(source, 2) * half + source // 2
        pltpu.make_async_copy(q_buf.at[place], q_buf.at[place], q_rsem.at[place]).wait()
        pltpu.make_async_copy(m_buf.at[place], m_buf.at[place], m_rsem.at[place]).wait()

    lane3 = lax.broadcasted_iota(jnp.int32, (n, 1, LANES), 2) // span
    absent = m_buf[...] - 1.0
    all_q = q_buf[...].astype(jnp.float32)
    for h in range(kv_heads):
        bias = jnp.where(lane3 == h, absent, 0.0)
        bias = jnp.broadcast_to(bias, (n, per_kv, LANES)).reshape(n * per_kv, LANES)
        q_aug[h, :, 0:hd] = all_q[:, h * per_kv:(h + 1) * per_kv, :].reshape(n * per_kv, hd).astype(jnp.bfloat16)
        q_aug[h, :, hd:hd + LANES] = bias.astype(jnp.bfloat16)

    def part_copy(j):
        return pltpu.make_async_remote_copy(
            src_ref=p_send.at[j], dst_ref=p_recv.at[pair],
            send_sem=p_ssem.at[j], recv_sem=p_rsem.at[pair],
            device_id=(seg, 2 * j + core), device_id_type=MESH)

    scale = math.log2(math.e) / math.sqrt(hd)
    lane = lax.broadcasted_iota(jnp.int32, (16, LANES), 1)
    units = per_kv // hpd

    @pl.loop(0, kv_heads)
    def _(h):
        keys = jnp.concatenate([k_buf[...], page_hot[...]], axis=1)
        values = jnp.concatenate([v_buf[...], jnp.ones((2 * tokens, LANES), jnp.bfloat16)], axis=1)
        for rb in range(n // 16):
            queries = q_aug[h, rb * 16 * per_kv:(rb + 1) * 16 * per_kv, :]
            scores = lax.dot_general(queries, keys, (((1,), (1,)), ((), ())),
                                     preferred_element_type=jnp.float32)
            top = jnp.max(scores, axis=1, keepdims=True) * scale
            weights = jnp.exp2(scores * scale - top).astype(jnp.bfloat16)
            sums = jnp.dot(weights, values, preferred_element_type=jnp.float32)
            o_scr[0] = sums[:, 0:hd] / sums[:, hd:]
            o_scr[1] = top + jnp.log2(sums[:, hd:])
            rows = slice(rb * 16, (rb + 1) * 16)
            for u in range(units):
                level = jnp.zeros((16, LANES), jnp.float32)
                for i in range(hpd):
                    index = u * hpd + i
                    value = o_scr[0, pl.ds(index, 16, stride=per_kv), :]
                    p_send[h * units + u, rows, i * hd:(i + 1) * hd] = value.astype(jnp.bfloat16)
                    level = jnp.where(lax.rem(lane, 32) == i, o_scr[1, pl.ds(index, 16, stride=per_kv), :], level)
                high = level.astype(jnp.bfloat16)
                rest = level - high.astype(jnp.float32)
                middle = rest.astype(jnp.bfloat16)
                low = rest - middle.astype(jnp.float32)
                packed = jnp.where(lane < 32, high.astype(jnp.float32),
                                   jnp.where(lane < 64, middle.astype(jnp.float32), low))
                p_send[h * units + u, rows, hpd * hd:hpd * hd + LANES] = packed.astype(jnp.bfloat16)
        for u in range(units):
            j = h * units + u

            @pl.when(j != pair)
            def _():
                part_copy(j).start()

            @pl.when(j == pair)
            def _():
                p_recv[pair] = p_send[j]

    @pl.loop(1, half)
    def _(k):
        source = lax.rem(pair + half - k, half)
        pltpu.make_async_copy(p_recv.at[source], p_recv.at[source], p_rsem.at[source]).wait()

    levels = []
    for j in range(half):
        packed = p_recv[j, :, hpd * hd:hpd * hd + LANES].astype(jnp.float32)
        levels.append(packed + pltpu.roll(packed, 96, 1) + pltpu.roll(packed, 64, 1))
    peak = functools.reduce(jnp.maximum, levels)
    factors = [jnp.exp2(level - peak) for level in levels]
    inverse = 1.0 / functools.reduce(jnp.add, factors)
    for i in range(hpd):
        total = jnp.zeros((n, hd), jnp.float32)
        for j in range(half):
            total += factors[j][:, i:i + 1] * p_recv[j, :, i * hd:(i + 1) * hd].astype(jnp.float32)
        att[:, i * hd:(i + 1) * hd] = (total * inverse[:, i:i + 1]).astype(jnp.bfloat16)

    def core_copy(k):
        return pltpu.make_async_remote_copy(
            src_ref=c_send.at[k], dst_ref=c_recv.at[k], send_sem=c_ssem.at[k], recv_sem=c_rsem.at[k],
            device_id=(seg, mate), device_id_type=MESH)

    def final_copy(j, k):
        return pltpu.make_async_remote_copy(
            src_ref=f_send.at[k, j], dst_ref=f_recv.at[k, pair],
            send_sem=f_ssem.at[k, j], recv_sem=f_rsem.at[k, pair],
            device_id=(ahead, 2 * j + core), device_id_type=MESH)

    @pl.loop(0, CHUNKS + 1)
    def _(step):
        @pl.when(step < CHUNKS)
        def _():
            weight_copy(step).wait()
            product = jnp.dot(att[...], w_buf[step], preferred_element_type=jnp.float32)
            own_sum[step, 0] = product[0:half]
            own_sum[step, 1] = product[half:n]
            other = own_sum[step, 1 - core]
            c_send[step] = jnp.concatenate(
                [other[:, 0:cols // 2], other[:, cols // 2:]], axis=0).astype(jnp.bfloat16)
            core_copy(step).start()

        @pl.when(step > 0)
        def _():
            k = step - 1
            core_copy(k).wait_recv()
            theirs = c_recv[k].astype(jnp.float32)
            both = own_sum[k, core] + jnp.concatenate([theirs[0:half], theirs[half:n]], axis=1)
            for b in range(blocks):
                t_scr[b * half:(b + 1) * half, :] = both[:, b * LANES:(b + 1) * LANES]
            for j in range(half):
                f_send[k, j] = t_scr[pl.ds(j, blocks, stride=half), :].astype(jnp.bfloat16)

            @pl.loop(0, half)
            def _(j):
                final_copy(lax.rem(pair + j, half), k).start()

    @pl.loop(0, CHUNKS)
    def _(k):
        @pl.loop(0, half)
        def _(j):
            pltpu.make_async_copy(f_recv.at[k, j], f_recv.at[k, j], f_rsem.at[k, j]).wait()

        total = f_recv[k, 0].astype(jnp.float32)
        for j in range(1, half):
            total += f_recv[k, j].astype(jnp.float32)
        out_ref[k] = total.astype(jnp.bfloat16)

    @pl.loop(1, n)
    def _(k):
        query_copy(k).wait_send()
        mask_copy(k).wait_send()

    @pl.loop(1, half)
    def _(k):
        part_copy(lax.rem(pair + k, half)).wait_send()

    @pl.loop(0, CHUNKS)
    def _(k):
        core_copy(k).wait_send()

        @pl.loop(0, half)
        def _(j):
            final_copy(j, k).wait_send()


def local(queries, page_ids, key_pages, value_pages, out_weight):
    n = lax.axis_size("dev")
    segments = lax.axis_size("segment")
    kv_heads, chosen = page_ids.shape[1:]
    pool, page, hd = key_pages.shape
    group = queries.shape[1] // (kv_heads * hd)
    depth, width = out_weight.shape
    half = n // 2
    hpd = kv_heads * group // n
    per_kv = group // 2
    tokens = pool * page
    cols = width // CHUNKS
    blocks = cols // LANES
    dims = (n, segments, kv_heads, chosen, pool, page, hd, group, width)
    bf16, f32 = jnp.bfloat16, jnp.float32
    dma = pltpu.SemaphoreType.DMA
    vmem = pltpu.VMEM
    out = pl.pallas_call(
        functools.partial(kernel, dims),
        out_shape=jax.ShapeDtypeStruct((CHUNKS, blocks, LANES), bf16),
        in_specs=[pl.BlockSpec(memory_space=pltpu.VMEM)] * 2 + [pl.BlockSpec(memory_space=pl.ANY)] * 3,
        out_specs=pl.BlockSpec(memory_space=pltpu.VMEM),
        scratch_shapes=[
            vmem((CHUNKS, depth, cols), bf16),
            vmem((2 * tokens, hd), bf16),
            vmem((2 * tokens, hd), bf16),
            vmem((2 * tokens, LANES), bf16),
            vmem((2, kv_heads * per_kv, hd), bf16),
            vmem((2, kv_heads * per_kv, hd), f32),
            vmem((half, 1, LANES), f32),
            vmem((n, kv_heads * per_kv, hd), bf16),
            vmem((n, 1, LANES), f32),
            vmem((kv_heads, n * per_kv, hd + LANES), bf16),
            vmem((2, 16 * per_kv, LANES), f32),
            vmem((half, n, hpd * hd + LANES), bf16),
            vmem((half, n, hpd * hd + LANES), bf16),
            vmem((n, hpd * hd), bf16),
            vmem((CHUNKS, 2, half, cols), f32),
            vmem((CHUNKS, n, cols // 2), bf16),
            vmem((CHUNKS, n, cols // 2), bf16),
            vmem((blocks * half, LANES), f32),
            vmem((CHUNKS, half, blocks, LANES), bf16),
            vmem((CHUNKS, half, blocks, LANES), bf16),
            dma((CHUNKS,)), dma((2,)), dma((2,)), dma((2,)),
            dma((n,)), dma((n,)), dma((n,)), dma((n,)),
            dma((half,)), dma((half,)),
            dma((CHUNKS,)), dma((CHUNKS,)),
            dma((CHUNKS, half)), dma((CHUNKS, half)),
        ],
        compiler_params=pltpu.CompilerParams(
            collective_id=0, has_side_effects=True, vmem_limit_bytes=56 * 1024 * 1024),
    )(queries, page_ids, key_pages.reshape(tokens, hd), value_pages.reshape(tokens, hd), out_weight)
    return out.reshape(1, width)


def solution(mesh):
    placed = (
        P(("segment", "dev"), None),
        P(("segment", "dev"), None, None),
        P(("segment", "dev"), None, None),
        P(("segment", "dev"), None, None),
        P(("segment", "dev"), None),
    )
    return jax.shard_map(
        local, mesh=mesh, in_specs=placed, out_specs=P(("segment", "dev"), None), check_vma=False
    )
```

time: 315 us -> 34.6 us (0.11)
  waiting for transfers between devices: 155 us -> 0 us
  blocking collectives: 82.9 us -> 0 us
  starting transfers between devices: 45.7 us -> 0 us
  Pallas kernels: 0 us -> 32.9 us
  local copies, waits for them, and re-layouts: 17.1 us -> 1.4 us
  matrix products: 10.1 us -> 0 us
  other arithmetic: 3.19 us -> 0 us
    all_to_all x3 -> x0, waiting for transfers between devices: 153 us -> none  [the longest x1 74.5 us: local(): lax.all_to_all(key_pages[asked_slots], 'dev', split_axis=0, concat_axis=0...]
    unnamed x1 -> x0, blocking collectives: 69.3 us -> none
    all_to_all x3 -> x0, starting transfers between devices: 44.1 us -> none  [the longest x1 19.8 us: local(): lax.all_to_all(value_pages[asked_slots], 'dev', split_axis=0, concat_axis...]
    pallas_call x0 -> x1, Pallas kernels: none -> 32.9 us  [local(): pl.pallas_call(functools.partial(kernel, dims), out_shape=jax.ShapeDtypeS...]
    all_to_all x1 -> x0, blocking collectives: 13.6 us -> none  [local(): lax.all_to_all(slot_table, 'dev', split_axis=0, concat_axis=0, tiled=True)]
    gather x4 -> x0, local copies, waits for them, and re-layouts: 12.4 us -> none  [the longest x1 3.15 us: local(): fetched_values.reshape(devices * capacity, page_tokens, head_dim)[target]]
    dot_general x3 -> x0, matrix products: 10.1 us -> none  [the longest x1 8.06 us: local(): jnp.dot(by_heads, out_weight, preferred_element_type=jnp.float32)]
  transfers between devices with their start and end apart: 4 -> 0, of which waited for: 4 -> 0; matrix products, arithmetic and copies ran while one was open for 3% -> 0% of each run, Pallas kernels for 0% -> 0%
where the time goes in v1:
time: 34.6 us; the launch traced here: 34.3 us
  Pallas kernels  32.9 us (95%)
  local copies, waits for them, and re-layouts  1.4 us (4%)
    pallas_call x1, Pallas kernels, local(): pl.pallas_call(functools.partial(kernel, dims), out_shape=jax.ShapeDtypeS...  32.9 us
    reshape x1, local copies, waits for them, and re-layouts, local(): return out.reshape(1, width)  1.4 us

profile of v1, /device:TPU:0, one launch (start us, length us, event | category | flops | bytes accessed | tf_op | source)
XLA Modules:
  0.0 34.3 jit_solution(10420452664671758756)
XLA Ops:
  0.0 32.9 %shard_map.55 = bf16[4,32,128]{2,1,0:T(8,128)(2,1)} custom-call(bf16[1,8192]{1,0:T(2,128)(2,1)} %q_ref.1, s32[1,4,32]{2,1,0:T(4,128)} %ids_ref.1, bf16[1024,128]{1,0:T(8,128)(2,1)} %bitcast.2, bf16[1024,128]{1,0:T(8,128)(2,1)} %bitcast.3, bf16[512,16384]{1,0:T(8,128)(2,1)} %weight_ref.1), custom_call_target="tpu_custom_call" | custom-call | tf_op jit(solution)/shard_map/pallas_call | solution.py:293
  32.9 1.4 %reshape.11 = bf16[1,16384]{1,0:T(2,128)(2,1)} reshape(bf16[4,32,128]{2,1,0:T(8,128)(2,1)} %shard_map.55) | data formatting | bytes 65536 | tf_op jit(solution)/shard_map/reshape | solution.py:328

commit v2 on v1

--- a/solution.py
+++ b/solution.py
@@ -15,12 +15,13 @@
 
 
 def kernel(dims, q_ref, ids_ref, key_ref, value_ref, weight_ref, out_ref,
-           w_buf, k_buf, v_buf, page_hot, q_stage, q32, m_stage, q_buf, m_buf, q_aug, o_scr,
-           p_send, p_recv, att, own_sum, c_send, c_recv, t_scr, f_send, f_recv,
-           w_sem, kv_sem, kv_send, kv_recv, q_ssem, q_rsem, m_ssem, m_rsem, p_ssem, p_rsem,
-           c_ssem, c_rsem, f_ssem, f_rsem):
+           q_in, ids_in, w_buf, k_buf, v_buf, key_t, q_stage, q32, m_stage, q_buf, m_buf, q_aug, o_scr,
+           p_send, p_recv, att, own_sum, c_send, c_recv, y_sum, y_send, y_recv, t_scr, f_send, f_recv,
+           in_sem, w_sem, kv_sem, kv_send, kv_recv, q_ssem, q_rsem, m_ssem, m_rsem, p_ssem, p_rsem,
+           c_ssem, c_rsem, y_ssem, y_rsem, f_ssem, f_rsem):
     n, segments, kv_heads, chosen, pool, page, hd, group, width = dims
     half = n // 2
+    quarter = half // 2
     hpd = kv_heads * group // n
     per_kv = group // 2
     tokens = pool * page
@@ -32,7 +33,10 @@
     core = lax.rem(me, 2)
     pair = me // 2
     mate = me + 1 - 2 * core
-    slot = core * half + pair
+    side = lax.rem(pair, 2)
+    level_of = pair // 2
+    across = 2 * (pair + 1 - 2 * side) + core
+    slot = core * half + side * quarter + level_of
     ahead = lax.rem(seg + 1, segments)
     behind = lax.rem(seg + segments - 1, segments)
 
@@ -40,15 +44,20 @@
         return pltpu.make_async_copy(
             weight_ref.at[:, pl.ds(pl.multiple_of(k * cols, cols), cols)], w_buf.at[k], w_sem.at[k])
 
+    query_in = pltpu.make_async_copy(q_ref, q_in, in_sem.at[0])
+    page_in = pltpu.make_async_copy(ids_ref, ids_in, in_sem.at[1])
+    query_in.start()
+    page_in.start()
+
     barrier = pltpu.get_barrier_semaphore()
 
     @pl.loop(1, n)
     def _(k):
         pl.semaphore_signal(barrier, inc=1, device_id=(seg, lax.rem(me + k, n)), device_id_type=MESH)
 
-    @pl.loop(0, half)
+    @pl.loop(0, quarter)
     def _(j):
-        pl.semaphore_signal(barrier, inc=1, device_id=(behind, 2 * j + core), device_id_type=MESH)
+        pl.semaphore_signal(barrier, inc=1, device_id=(behind, 4 * j + 2 * side + core), device_id_type=MESH)
 
     here = pl.ds(pl.multiple_of(core * tokens, tokens), tokens)
     key_local = pltpu.make_async_copy(key_ref, k_buf.at[here], kv_sem.at[0])
@@ -59,6 +68,9 @@
     @pl.loop(0, CHUNKS)
     def _(k):
         weight_copy(k).start()
+
+    query_in.wait()
+    page_in.wait()
 
     for c in range(2):
         for h in range(kv_heads):
@@ -66,12 +78,12 @@
                 for i in range(hpd):
                     head = h * group + u * 2 * hpd + c * hpd + i
                     place = h * per_kv + u * hpd + i
-                    q32[c, place:place + 1, :] = q_ref[0:1, head * hd:(head + 1) * hd].astype(jnp.float32)
+                    q32[c, place:place + 1, :] = q_in[0:1, head * hd:(head + 1) * hd].astype(jnp.float32)
     q_stage[...] = q32[...].astype(jnp.bfloat16)
 
     head_of_lane = lax.broadcasted_iota(jnp.int32, (kv_heads, LANES), 1) // span
     pick = (head_of_lane == lax.broadcasted_iota(jnp.int32, (kv_heads, LANES), 0)).astype(jnp.float32)
-    ids = ids_ref[0].astype(jnp.float32)
+    ids = ids_in[0].astype(jnp.float32)
     spread = lax.dot_general(ids, pick, (((0,), (0,)), ((), ())),
                              precision=lax.Precision.HIGHEST, preferred_element_type=jnp.float32)
     in_span = lax.rem(lax.broadcasted_iota(jnp.int32, (chosen, LANES), 1), span).astype(jnp.float32)
@@ -83,7 +95,14 @@
     q_buf[slot] = q_stage[core]
     m_buf[slot] = m_stage[pair]
 
-    pl.semaphore_wait(barrier, n - 1 + half)
+    key_local.wait()
+    value_local.wait()
+    lane_page = lax.rem(lax.broadcasted_iota(jnp.int32, (LANES, 2 * tokens), 0), span)
+    token_page = lax.broadcasted_iota(jnp.int32, (LANES, 2 * tokens), 1) // page
+    key_t[hd:hd + LANES, :] = jnp.where(lane_page == token_page, BIG, 0.0).astype(jnp.bfloat16)
+    key_t[0:hd, here] = k_buf[here, :].T
+
+    pl.semaphore_wait(barrier, n - 1 + quarter)
 
     def query_copy(k):
         peer = lax.rem(me + k, n)
@@ -99,33 +118,29 @@
             send_sem=m_ssem.at[k], recv_sem=m_rsem.at[slot],
             device_id=(seg, peer), device_id_type=MESH)
 
-    @pl.loop(1, n)
-    def _(k):
-        query_copy(k).start()
-        mask_copy(k).start()
-
     key_remote = pltpu.make_async_remote_copy(
-        src_ref=key_ref, dst_ref=k_buf.at[here], send_sem=kv_send.at[0], recv_sem=kv_recv.at[0],
+        src_ref=k_buf.at[here], dst_ref=k_buf.at[here], send_sem=kv_send.at[0], recv_sem=kv_recv.at[0],
         device_id=(seg, mate), device_id_type=MESH)
     value_remote = pltpu.make_async_remote_copy(
-        src_ref=value_ref, dst_ref=v_buf.at[here], send_sem=kv_send.at[1], recv_sem=kv_recv.at[1],
+        src_ref=v_buf.at[here], dst_ref=v_buf.at[here], send_sem=kv_send.at[1], recv_sem=kv_recv.at[1],
         device_id=(seg, mate), device_id_type=MESH)
     key_remote.start()
     value_remote.start()
 
-    lane_page = lax.rem(lax.broadcasted_iota(jnp.int32, (2 * tokens, LANES), 1), span)
-    token_page = lax.broadcasted_iota(jnp.int32, (2 * tokens, LANES), 0) // page
-    page_hot[...] = jnp.where(lane_page == token_page, BIG, 0.0).astype(jnp.bfloat16)
-
-    key_local.wait()
-    value_local.wait()
+    @pl.loop(1, n)
+    def _(k):
+        query_copy(k).start()
+        mask_copy(k).start()
+
     key_remote.wait()
+    there = pl.ds(pl.multiple_of((1 - core) * tokens, tokens), tokens)
+    key_t[0:hd, there] = k_buf[there, :].T
     value_remote.wait()
 
     @pl.loop(1, n)
     def _(k):
         source = lax.rem(me + n - k, n)
-        place = lax.rem(source, 2) * half + source // 2
+        place = lax.rem(source, 2) * half + lax.rem(source // 2, 2) * quarter + source // 4
         pltpu.make_async_copy(q_buf.at[place], q_buf.at[place], q_rsem.at[place]).wait()
         pltpu.make_async_copy(m_buf.at[place], m_buf.at[place], m_rsem.at[place]).wait()
 
@@ -148,14 +163,16 @@
     lane = lax.broadcasted_iota(jnp.int32, (16, LANES), 1)
     units = per_kv // hpd
 
-    @pl.loop(0, kv_heads)
-    def _(h):
-        keys = jnp.concatenate([k_buf[...], page_hot[...]], axis=1)
-        values = jnp.concatenate([v_buf[...], jnp.ones((2 * tokens, LANES), jnp.bfloat16)], axis=1)
-        for rb in range(n // 16):
-            queries = q_aug[h, rb * 16 * per_kv:(rb + 1) * 16 * per_kv, :]
-            scores = lax.dot_general(queries, keys, (((1,), (1,)), ((), ())),
-                                     preferred_element_type=jnp.float32)
+    tiles = [(h, rb) for h in range(kv_heads) for rb in range(n // 16)]
+
+    def score(h, rb):
+        queries = q_aug[h, rb * 16 * per_kv:(rb + 1) * 16 * per_kv, :]
+        return jnp.dot(queries, key_t[...], preferred_element_type=jnp.float32)
+
+    values = jnp.concatenate([v_buf[...], jnp.ones((2 * tokens, LANES), jnp.bfloat16)], axis=1)
+    scores = score(*tiles[0])
+    for index_of, (h, rb) in enumerate(tiles):
+            upcoming = score(*tiles[index_of + 1]) if index_of + 1 < len(tiles) else None
             top = jnp.max(scores, axis=1, keepdims=True) * scale
             weights = jnp.exp2(scores * scale - top).astype(jnp.bfloat16)
             sums = jnp.dot(weights, values, preferred_element_type=jnp.float32)
@@ -176,16 +193,24 @@
                 packed = jnp.where(lane < 32, high.astype(jnp.float32),
                                    jnp.where(lane < 64, middle.astype(jnp.float32), low))
                 p_send[h * units + u, rows, hpd * hd:hpd * hd + LANES] = packed.astype(jnp.bfloat16)
-        for u in range(units):
-            j = h * units + u
-
-            @pl.when(j != pair)
-            def _():
-                part_copy(j).start()
-
-            @pl.when(j == pair)
-            def _():
-                p_recv[pair] = p_send[j]
+            scores = upcoming
+            if rb + 1 < n // 16:
+                continue
+            for u in range(units):
+                j = h * units + u
+
+                @pl.when(j != pair)
+                def _(j=j):
+                    part_copy(j).start()
+
+                @pl.when(j == pair)
+                def _(j=j):
+                    p_recv[pair] = p_send[j]
+
+    @pl.loop(1, n)
+    def _(k):
+        query_copy(k).wait_send()
+        mask_copy(k).wait_send()
 
     @pl.loop(1, half)
     def _(k):
@@ -210,13 +235,21 @@
             src_ref=c_send.at[k], dst_ref=c_recv.at[k], send_sem=c_ssem.at[k], recv_sem=c_rsem.at[k],
             device_id=(seg, mate), device_id_type=MESH)
 
+    def side_copy(k):
+        return pltpu.make_async_remote_copy(
+            src_ref=y_send.at[k], dst_ref=y_recv.at[k], send_sem=y_ssem.at[k], recv_sem=y_rsem.at[k],
+            device_id=(seg, across), device_id_type=MESH)
+
     def final_copy(j, k):
         return pltpu.make_async_remote_copy(
-            src_ref=f_send.at[k, j], dst_ref=f_recv.at[k, pair],
-            send_sem=f_ssem.at[k, j], recv_sem=f_rsem.at[k, pair],
-            device_id=(ahead, 2 * j + core), device_id_type=MESH)
-
-    @pl.loop(0, CHUNKS + 1)
+            src_ref=f_send.at[k, j], dst_ref=f_recv.at[k, level_of],
+            send_sem=f_ssem.at[k, j], recv_sem=f_rsem.at[k, level_of],
+            device_id=(ahead, 4 * j + 2 * side + core), device_id_type=MESH)
+
+    pieces = max(1, 16 // quarter)
+    piece = cols // pieces
+
+    @pl.loop(0, CHUNKS + 2)
     def _(step):
         @pl.when(step < CHUNKS)
         def _():
@@ -229,47 +262,56 @@
                 [other[:, 0:cols // 2], other[:, cols // 2:]], axis=0).astype(jnp.bfloat16)
             core_copy(step).start()
 
-        @pl.when(step > 0)
+        @pl.when((step > 0) & (step <= CHUNKS))
         def _():
             k = step - 1
             core_copy(k).wait_recv()
             theirs = c_recv[k].astype(jnp.float32)
             both = own_sum[k, core] + jnp.concatenate([theirs[0:half], theirs[half:n]], axis=1)
+            y_sum[k, 0] = both[0:quarter]
+            y_sum[k, 1] = both[quarter:half]
+            other = y_sum[k, 1 - side]
+            y_send[k] = jnp.concatenate(
+                [other[:, p * piece:(p + 1) * piece] for p in range(pieces)], axis=0).astype(jnp.bfloat16)
+            side_copy(k).start()
+
+        @pl.when(step > 1)
+        def _():
+            k = step - 2
+            side_copy(k).wait_recv()
+            theirs = y_recv[k].astype(jnp.float32)
+            both = y_sum[k, side] + jnp.concatenate(
+                [theirs[p * quarter:(p + 1) * quarter] for p in range(pieces)], axis=1)
             for b in range(blocks):
-                t_scr[b * half:(b + 1) * half, :] = both[:, b * LANES:(b + 1) * LANES]
-            for j in range(half):
-                f_send[k, j] = t_scr[pl.ds(j, blocks, stride=half), :].astype(jnp.bfloat16)
-
-            @pl.loop(0, half)
+                t_scr[b * quarter:(b + 1) * quarter, :] = both[:, b * LANES:(b + 1) * LANES]
+            for j in range(quarter):
+                f_send[k, j] = t_scr[pl.ds(j, blocks, stride=quarter), :].astype(jnp.bfloat16)
+
+            @pl.loop(0, quarter)
             def _(j):
-                final_copy(lax.rem(pair + j, half), k).start()
+                final_copy(lax.rem(level_of + 1 + j, quarter), k).start()
+
+    @pl.loop(1, half)
+    def _(k):
+        part_copy(lax.rem(pair + k, half)).wait_send()
 
     @pl.loop(0, CHUNKS)
     def _(k):
-        @pl.loop(0, half)
-        def _(j):
+        core_copy(k).wait_send()
+        side_copy(k).wait_send()
+
+    for k in range(CHUNKS):
+        @pl.loop(0, quarter)
+        def _(j, k=k):
             pltpu.make_async_copy(f_recv.at[k, j], f_recv.at[k, j], f_rsem.at[k, j]).wait()
 
         total = f_recv[k, 0].astype(jnp.float32)
-        for j in range(1, half):
+        for j in range(1, quarter):
             total += f_recv[k, j].astype(jnp.float32)
         out_ref[k] = total.astype(jnp.bfloat16)
 
-    @pl.loop(1, n)
-    def _(k):
-        query_copy(k).wait_send()
-        mask_copy(k).wait_send()
-
-    @pl.loop(1, half)
-    def _(k):
-        part_copy(lax.rem(pair + k, half)).wait_send()
-
-    @pl.loop(0, CHUNKS)
-    def _(k):
-        core_copy(k).wait_send()
-
-        @pl.loop(0, half)
-        def _(j):
+        @pl.loop(0, quarter)
+        def _(j, k=k):
             final_copy(j, k).wait_send()
 
 
@@ -281,6 +323,8 @@
     group = queries.shape[1] // (kv_heads * hd)
     depth, width = out_weight.shape
     half = n // 2
+    quarter = half // 2
+    pieces = max(1, 16 // quarter)
     hpd = kv_heads * group // n
     per_kv = group // 2
     tokens = pool * page
@@ -293,13 +337,15 @@
     out = pl.pallas_call(
         functools.partial(kernel, dims),
         out_shape=jax.ShapeDtypeStruct((CHUNKS, blocks, LANES), bf16),
-        in_specs=[pl.BlockSpec(memory_space=pltpu.VMEM)] * 2 + [pl.BlockSpec(memory_space=pl.ANY)] * 3,
+        in_specs=[pl.BlockSpec(memory_space=pl.ANY)] * 5,
         out_specs=pl.BlockSpec(memory_space=pltpu.VMEM),
         scratch_shapes=[
+            vmem(queries.shape, bf16),
+            vmem(page_ids.shape, jnp.int32),
             vmem((CHUNKS, depth, cols), bf16),
             vmem((2 * tokens, hd), bf16),
             vmem((2 * tokens, hd), bf16),
-            vmem((2 * tokens, LANES), bf16),
+            vmem((hd + LANES, 2 * tokens), bf16),
             vmem((2, kv_heads * per_kv, hd), bf16),
             vmem((2, kv_heads * per_kv, hd), f32),
             vmem((half, 1, LANES), f32),
@@ -313,14 +359,17 @@
             vmem((CHUNKS, 2, half, cols), f32),
             vmem((CHUNKS, n, cols // 2), bf16),
             vmem((CHUNKS, n, cols // 2), bf16),
-            vmem((blocks * half, LANES), f32),
-            vmem((CHUNKS, half, blocks, LANES), bf16),
-            vmem((CHUNKS, half, blocks, LANES), bf16),
-            dma((CHUNKS,)), dma((2,)), dma((2,)), dma((2,)),
+            vmem((CHUNKS, 2, quarter, cols), f32),
+            vmem((CHUNKS, pieces * quarter, cols // pieces), bf16),
+            vmem((CHUNKS, pieces * quarter, cols // pieces), bf16),
+            vmem((blocks * quarter, LANES), f32),
+            vmem((CHUNKS, quarter, blocks, LANES), bf16),
+            vmem((CHUNKS, quarter, blocks, LANES), bf16),
+            dma((2,)), dma((CHUNKS,)), dma((2,)), dma((2,)), dma((2,)),
             dma((n,)), dma((n,)), dma((n,)), dma((n,)),
             dma((half,)), dma((half,)),
-            dma((CHUNKS,)), dma((CHUNKS,)),
-            dma((CHUNKS, half)), dma((CHUNKS, half)),
+            dma((CHUNKS,)), dma((CHUNKS,)), dma((CHUNKS,)), dma((CHUNKS,)),
+            dma((CHUNKS, quarter)), dma((CHUNKS, quarter)),
         ],
         compiler_params=pltpu.CompilerParams(
             collective_id=0, has_side_effects=True, vmem_limit_bytes=56 * 1024 * 1024),

time: 34.6 us -> 35.9 us (1.038)
  Pallas kernels: 32.9 us -> 34.3 us
    pallas_call x1, Pallas kernels: 32.9 us -> 34.3 us  [local(): pl.pallas_call(functools.partial(kernel, dims), out_shape=jax.ShapeDtypeS...]
where the time goes in v2:
time: 35.9 us; the launch traced here: 35.7 us
  Pallas kernels  34.3 us (96%)
  local copies, waits for them, and re-layouts  1.4 us (4%)
    pallas_call x1, Pallas kernels, local(): pl.pallas_call(functools.partial(kernel, dims), out_shape=jax.ShapeDtypeS...  34.3 us
    reshape x1, local copies, waits for them, and re-layouts, local(): return out.reshape(1, width)  1.4 us

profile of v2, /device:TPU:0, one launch (start us, length us, event | category | flops | bytes accessed | tf_op | source)
XLA Modules:
  0.0 35.7 jit_solution(12207054212834201825)
XLA Ops:
  0.0 34.3 %shard_map.55 = bf16[4,32,128]{2,1,0:T(8,128)(2,1)} custom-call(bf16[1,8192]{1,0:T(2,128)(2,1)} %q_ref.1, s32[1,4,32]{2,1,0:T(4,128)} %ids_ref.1, bf16[1024,128]{1,0:T(8,128)(2,1)} %bitcast.2, bf16[1024,128]{1,0:T(8,128)(2,1)} %bitcast.3, bf16[512,16384]{1,0:T(8,128)(2,1)} %weight_ref.1), custom_call_target="tpu_custom_call" | custom-call | tf_op jit(solution)/shard_map/pallas_call | solution.py:337
  34.3 1.4 %reshape.11 = bf16[1,16384]{1,0:T(2,128)(2,1)} reshape(bf16[4,32,128]{2,1,0:T(8,128)(2,1)} %shard_map.55) | data formatting | bytes 65536 | tf_op jit(solution)/shard_map/reshape | solution.py:377

commit v3 on v2

--- a/solution.py
+++ b/solution.py
@@ -65,12 +65,7 @@
     key_local.start()
     value_local.start()
 
-    @pl.loop(0, CHUNKS)
-    def _(k):
-        weight_copy(k).start()
-
     query_in.wait()
-    page_in.wait()
 
     for c in range(2):
         for h in range(kv_heads):
@@ -80,6 +75,43 @@
                     place = h * per_kv + u * hpd + i
                     q32[c, place:place + 1, :] = q_in[0:1, head * hd:(head + 1) * hd].astype(jnp.float32)
     q_stage[...] = q32[...].astype(jnp.bfloat16)
+
+    q_buf[slot] = q_stage[core]
+
+    pl.semaphore_wait(barrier, n - 1 + quarter)
+
+    key_remote = pltpu.make_async_remote_copy(
+        src_ref=key_ref, dst_ref=k_buf.at[here], send_sem=kv_send.at[0], recv_sem=kv_recv.at[0],
+        device_id=(seg, mate), device_id_type=MESH)
+    value_remote = pltpu.make_async_remote_copy(
+        src_ref=value_ref, dst_ref=v_buf.at[here], send_sem=kv_send.at[1], recv_sem=kv_recv.at[1],
+        device_id=(seg, mate), device_id_type=MESH)
+    key_remote.start()
+    value_remote.start()
+
+    def query_copy(k):
+        peer = lax.rem(me + k, n)
+        return pltpu.make_async_remote_copy(
+            src_ref=q_stage.at[lax.rem(peer, 2)], dst_ref=q_buf.at[slot],
+            send_sem=q_ssem.at[k], recv_sem=q_rsem.at[slot],
+            device_id=(seg, peer), device_id_type=MESH)
+
+    def mask_copy(k):
+        peer = lax.rem(me + k, n)
+        return pltpu.make_async_remote_copy(
+            src_ref=m_stage.at[peer // 2], dst_ref=m_buf.at[slot],
+            send_sem=m_ssem.at[k], recv_sem=m_rsem.at[slot],
+            device_id=(seg, peer), device_id_type=MESH)
+
+    @pl.loop(1, n)
+    def _(k):
+        query_copy(k).start()
+
+    @pl.loop(0, CHUNKS)
+    def _(k):
+        weight_copy(k).start()
+
+    page_in.wait()
 
     head_of_lane = lax.broadcasted_iota(jnp.int32, (kv_heads, LANES), 1) // span
     pick = (head_of_lane == lax.broadcasted_iota(jnp.int32, (kv_heads, LANES), 0)).astype(jnp.float32)
@@ -92,45 +124,18 @@
         hit = (jnp.abs(offset - float(j * span)) < 0.5).astype(jnp.float32)
         m_stage[j] = jnp.max(hit, axis=0, keepdims=True)
 
-    q_buf[slot] = q_stage[core]
     m_buf[slot] = m_stage[pair]
+
+    @pl.loop(1, n)
+    def _(k):
+        mask_copy(k).start()
 
     key_local.wait()
     value_local.wait()
-    lane_page = lax.rem(lax.broadcasted_iota(jnp.int32, (LANES, 2 * tokens), 0), span)
-    token_page = lax.broadcasted_iota(jnp.int32, (LANES, 2 * tokens), 1) // page
+    lane_page = lax.rem(lax.broadcasted_iota(jnp.int32, (LANES, LANES), 0), span)[:, 0:1]
+    token_page = lax.broadcasted_iota(jnp.int32, (8, 2 * tokens), 1)[0:1] // page
     key_t[hd:hd + LANES, :] = jnp.where(lane_page == token_page, BIG, 0.0).astype(jnp.bfloat16)
     key_t[0:hd, here] = k_buf[here, :].T
-
-    pl.semaphore_wait(barrier, n - 1 + quarter)
-
-    def query_copy(k):
-        peer = lax.rem(me + k, n)
-        return pltpu.make_async_remote_copy(
-            src_ref=q_stage.at[lax.rem(peer, 2)], dst_ref=q_buf.at[slot],
-            send_sem=q_ssem.at[k], recv_sem=q_rsem.at[slot],
-            device_id=(seg, peer), device_id_type=MESH)
-
-    def mask_copy(k):
-        peer = lax.rem(me + k, n)
-        return pltpu.make_async_remote_copy(
-            src_ref=m_stage.at[peer // 2], dst_ref=m_buf.at[slot],
-            send_sem=m_ssem.at[k], recv_sem=m_rsem.at[slot],
-            device_id=(seg, peer), device_id_type=MESH)
-
-    key_remote = pltpu.make_async_remote_copy(
-        src_ref=k_buf.at[here], dst_ref=k_buf.at[here], send_sem=kv_send.at[0], recv_sem=kv_recv.at[0],
-        device_id=(seg, mate), device_id_type=MESH)
-    value_remote = pltpu.make_async_remote_copy(
-        src_ref=v_buf.at[here], dst_ref=v_buf.at[here], send_sem=kv_send.at[1], recv_sem=kv_recv.at[1],
-        device_id=(seg, mate), device_id_type=MESH)
-    key_remote.start()
-    value_remote.start()
-
-    @pl.loop(1, n)
-    def _(k):
-        query_copy(k).start()
-        mask_copy(k).start()
 
     key_remote.wait()
     there = pl.ds(pl.multiple_of((1 - core) * tokens, tokens), tokens)
@@ -163,16 +168,12 @@
     lane = lax.broadcasted_iota(jnp.int32, (16, LANES), 1)
     units = per_kv // hpd
 
-    tiles = [(h, rb) for h in range(kv_heads) for rb in range(n // 16)]
-
-    def score(h, rb):
-        queries = q_aug[h, rb * 16 * per_kv:(rb + 1) * 16 * per_kv, :]
-        return jnp.dot(queries, key_t[...], preferred_element_type=jnp.float32)
-
-    values = jnp.concatenate([v_buf[...], jnp.ones((2 * tokens, LANES), jnp.bfloat16)], axis=1)
-    scores = score(*tiles[0])
-    for index_of, (h, rb) in enumerate(tiles):
-            upcoming = score(*tiles[index_of + 1]) if index_of + 1 < len(tiles) else None
+    @pl.loop(0, kv_heads)
+    def _(h):
+        values = jnp.concatenate([v_buf[...], jnp.ones((2 * tokens, LANES), jnp.bfloat16)], axis=1)
+        for rb in range(n // 16):
+            queries = q_aug[h, rb * 16 * per_kv:(rb + 1) * 16 * per_kv, :]
+            scores = jnp.dot(queries, key_t[...], preferred_element_type=jnp.float32)
             top = jnp.max(scores, axis=1, keepdims=True) * scale
             weights = jnp.exp2(scores * scale - top).astype(jnp.bfloat16)
             sums = jnp.dot(weights, values, preferred_element_type=jnp.float32)
@@ -193,19 +194,16 @@
                 packed = jnp.where(lane < 32, high.astype(jnp.float32),
                                    jnp.where(lane < 64, middle.astype(jnp.float32), low))
                 p_send[h * units + u, rows, hpd * hd:hpd * hd + LANES] = packed.astype(jnp.bfloat16)
-            scores = upcoming
-            if rb + 1 < n // 16:
-                continue
-            for u in range(units):
-                j = h * units + u
-
-                @pl.when(j != pair)
-                def _(j=j):
-                    part_copy(j).start()
-
-                @pl.when(j == pair)
-                def _(j=j):
-                    p_recv[pair] = p_send[j]
+        for u in range(units):
+            j = h * units + u
+
+            @pl.when(j != pair)
+            def _():
+                part_copy(j).start()
+
+            @pl.when(j == pair)
+            def _():
+                p_recv[pair] = p_send[j]
 
     @pl.loop(1, n)
     def _(k):

time: 35.9 us -> 37.1 us (1.033)
  Pallas kernels: 34.3 us -> 35.5 us
    pallas_call x1, Pallas kernels: 34.3 us -> 35.5 us  [local(): pl.pallas_call(functools.partial(kernel, dims), out_shape=jax.ShapeDtypeS...]
where the time goes in v3:
time: 37.1 us; the launch traced here: 36.9 us
  Pallas kernels  35.5 us (96%)
  local copies, waits for them, and re-layouts  1.4 us (4%)
    pallas_call x1, Pallas kernels, local(): pl.pallas_call(functools.partial(kernel, dims), out_shape=jax.ShapeDtypeS...  35.5 us
    reshape x1, local copies, waits for them, and re-layouts, local(): return out.reshape(1, width)  1.4 us

profile of v3, /device:TPU:0, one launch (start us, length us, event | category | flops | bytes accessed | tf_op | source)
XLA Modules:
  0.0 36.9 jit_solution(11733462506587323715)
XLA Ops:
  0.0 35.5 %shard_map.55 = bf16[4,32,128]{2,1,0:T(8,128)(2,1)} custom-call(bf16[1,8192]{1,0:T(2,128)(2,1)} %q_ref.1, s32[1,4,32]{2,1,0:T(4,128)} %ids_ref.1, bf16[1024,128]{1,0:T(8,128)(2,1)} %bitcast.2, bf16[1024,128]{1,0:T(8,128)(2,1)} %bitcast.3, bf16[512,16384]{1,0:T(8,128)(2,1)} %weight_ref.1), custom_call_target="tpu_custom_call" | custom-call | tf_op jit(solution)/shard_map/pallas_call | solution.py:335
  35.5 1.4 %reshape.11 = bf16[1,16384]{1,0:T(2,128)(2,1)} reshape(bf16[4,32,128]{2,1,0:T(8,128)(2,1)} %shard_map.55) | data formatting | bytes 65536 | tf_op jit(solution)/shard_map/reshape | solution.py:375

commit v4 on v1

--- a/solution.py
+++ b/solution.py
@@ -15,9 +15,9 @@
 
 
 def kernel(dims, q_ref, ids_ref, key_ref, value_ref, weight_ref, out_ref,
-           w_buf, k_buf, v_buf, page_hot, q_stage, q32, m_stage, q_buf, m_buf, q_aug, o_scr,
+           q_in, ids_in, w_buf, k_buf, v_buf, page_hot, q_stage, q32, m_stage, q_buf, m_buf, q_aug, o_scr,
            p_send, p_recv, att, own_sum, c_send, c_recv, t_scr, f_send, f_recv,
-           w_sem, kv_sem, kv_send, kv_recv, q_ssem, q_rsem, m_ssem, m_rsem, p_ssem, p_rsem,
+           in_sem, w_sem, kv_sem, kv_send, kv_recv, q_ssem, q_rsem, m_ssem, m_rsem, p_ssem, p_rsem,
            c_ssem, c_rsem, f_ssem, f_rsem):
     n, segments, kv_heads, chosen, pool, page, hd, group, width = dims
     half = n // 2
@@ -40,6 +40,11 @@
         return pltpu.make_async_copy(
             weight_ref.at[:, pl.ds(pl.multiple_of(k * cols, cols), cols)], w_buf.at[k], w_sem.at[k])
 
+    query_in = pltpu.make_async_copy(q_ref, q_in, in_sem.at[0])
+    page_in = pltpu.make_async_copy(ids_ref, ids_in, in_sem.at[1])
+    query_in.start()
+    page_in.start()
+
     barrier = pltpu.get_barrier_semaphore()
 
     @pl.loop(1, n)
@@ -59,6 +64,9 @@
     @pl.loop(0, CHUNKS)
     def _(k):
         weight_copy(k).start()
+
+    query_in.wait()
+    page_in.wait()
 
     for c in range(2):
         for h in range(kv_heads):
@@ -66,12 +74,12 @@
                 for i in range(hpd):
                     head = h * group + u * 2 * hpd + c * hpd + i
                     place = h * per_kv + u * hpd + i
-                    q32[c, place:place + 1, :] = q_ref[0:1, head * hd:(head + 1) * hd].astype(jnp.float32)
+                    q32[c, place:place + 1, :] = q_in[0:1, head * hd:(head + 1) * hd].astype(jnp.float32)
     q_stage[...] = q32[...].astype(jnp.bfloat16)
 
     head_of_lane = lax.broadcasted_iota(jnp.int32, (kv_heads, LANES), 1) // span
     pick = (head_of_lane == lax.broadcasted_iota(jnp.int32, (kv_heads, LANES), 0)).astype(jnp.float32)
-    ids = ids_ref[0].astype(jnp.float32)
+    ids = ids_in[0].astype(jnp.float32)
     spread = lax.dot_general(ids, pick, (((0,), (0,)), ((), ())),
                              precision=lax.Precision.HIGHEST, preferred_element_type=jnp.float32)
     in_span = lax.rem(lax.broadcasted_iota(jnp.int32, (chosen, LANES), 1), span).astype(jnp.float32)
@@ -104,21 +112,21 @@
         query_copy(k).start()
         mask_copy(k).start()
 
+    key_local.wait()
+    value_local.wait()
     key_remote = pltpu.make_async_remote_copy(
-        src_ref=key_ref, dst_ref=k_buf.at[here], send_sem=kv_send.at[0], recv_sem=kv_recv.at[0],
+        src_ref=k_buf.at[here], dst_ref=k_buf.at[here], send_sem=kv_send.at[0], recv_sem=kv_recv.at[0],
         device_id=(seg, mate), device_id_type=MESH)
     value_remote = pltpu.make_async_remote_copy(
-        src_ref=value_ref, dst_ref=v_buf.at[here], send_sem=kv_send.at[1], recv_sem=kv_recv.at[1],
+        src_ref=v_buf.at[here], dst_ref=v_buf.at[here], send_sem=kv_send.at[1], recv_sem=kv_recv.at[1],
         device_id=(seg, mate), device_id_type=MESH)
     key_remote.start()
     value_remote.start()
 
-    lane_page = lax.rem(lax.broadcasted_iota(jnp.int32, (2 * tokens, LANES), 1), span)
+    lane_page = lax.rem(lax.broadcasted_iota(jnp.int32, (8, LANES), 1), span)[0:1]
     token_page = lax.broadcasted_iota(jnp.int32, (2 * tokens, LANES), 0) // page
     page_hot[...] = jnp.where(lane_page == token_page, BIG, 0.0).astype(jnp.bfloat16)
 
-    key_local.wait()
-    value_local.wait()
     key_remote.wait()
     value_remote.wait()
 
@@ -187,6 +195,11 @@
             def _():
                 p_recv[pair] = p_send[j]
 
+    @pl.loop(1, n)
+    def _(k):
+        query_copy(k).wait_send()
+        mask_copy(k).wait_send()
+
     @pl.loop(1, half)
     def _(k):
         source = lax.rem(pair + half - k, half)
@@ -244,6 +257,14 @@
             def _(j):
                 final_copy(lax.rem(pair + j, half), k).start()
 
+    @pl.loop(1, half)
+    def _(k):
+        part_copy(lax.rem(pair + k, half)).wait_send()
+
+    @pl.loop(0, CHUNKS)
+    def _(k):
+        core_copy(k).wait_send()
+
     @pl.loop(0, CHUNKS)
     def _(k):
         @pl.loop(0, half)
@@ -255,19 +276,8 @@
             total += f_recv[k, j].astype(jnp.float32)
         out_ref[k] = total.astype(jnp.bfloat16)
 
-    @pl.loop(1, n)
-    def _(k):
-        query_copy(k).wait_send()
-        mask_copy(k).wait_send()
-
-    @pl.loop(1, half)
-    def _(k):
-        part_copy(lax.rem(pair + k, half)).wait_send()
-
     @pl.loop(0, CHUNKS)
     def _(k):
-        core_copy(k).wait_send()
-
         @pl.loop(0, half)
         def _(j):
             final_copy(j, k).wait_send()
@@ -293,9 +303,11 @@
     out = pl.pallas_call(
         functools.partial(kernel, dims),
         out_shape=jax.ShapeDtypeStruct((CHUNKS, blocks, LANES), bf16),
-        in_specs=[pl.BlockSpec(memory_space=pltpu.VMEM)] * 2 + [pl.BlockSpec(memory_space=pl.ANY)] * 3,
+        in_specs=[pl.BlockSpec(memory_space=pl.ANY)] * 5,
         out_specs=pl.BlockSpec(memory_space=pltpu.VMEM),
         scratch_shapes=[
+            vmem(queries.shape, bf16),
+            vmem(page_ids.shape, jnp.int32),
             vmem((CHUNKS, depth, cols), bf16),
             vmem((2 * tokens, hd), bf16),
             vmem((2 * tokens, hd), bf16),
@@ -316,7 +328,7 @@
             vmem((blocks * half, LANES), f32),
             vmem((CHUNKS, half, blocks, LANES), bf16),
             vmem((CHUNKS, half, blocks, LANES), bf16),
-            dma((CHUNKS,)), dma((2,)), dma((2,)), dma((2,)),
+            dma((2,)), dma((CHUNKS,)), dma((2,)), dma((2,)), dma((2,)),
             dma((n,)), dma((n,)), dma((n,)), dma((n,)),
             dma((half,)), dma((half,)),
             dma((CHUNKS,)), dma((CHUNKS,)),

time: 34.6 us -> 33.6 us (0.971)
  Pallas kernels: 32.9 us -> 32 us
    pallas_call x1, Pallas kernels: 32.9 us -> 32 us  [local(): pl.pallas_call(functools.partial(kernel, dims), out_shape=jax.ShapeDtypeS...]
where the time goes in v4:
time: 33.6 us; the launch traced here: 33.4 us
  Pallas kernels  32 us (95%)
  local copies, waits for them, and re-layouts  1.4 us (4%)
    pallas_call x1, Pallas kernels, local(): pl.pallas_call(functools.partial(kernel, dims), out_shape=jax.ShapeDtypeS...  32 us
    reshape x1, local copies, waits for them, and re-layouts, local(): return out.reshape(1, width)  1.4 us

profile of v4, /device:TPU:0, one launch (start us, length us, event | category | flops | bytes accessed | tf_op | source)
XLA Modules:
  0.0 33.4 jit_solution(14534554436771333358)
XLA Ops:
  0.0 32.0 %shard_map.55 = bf16[4,32,128]{2,1,0:T(8,128)(2,1)} custom-call(bf16[1,8192]{1,0:T(2,128)(2,1)} %q_ref.1, s32[1,4,32]{2,1,0:T(4,128)} %ids_ref.1, bf16[1024,128]{1,0:T(8,128)(2,1)} %bitcast.2, bf16[1024,128]{1,0:T(8,128)(2,1)} %bitcast.3, bf16[512,16384]{1,0:T(8,128)(2,1)} %weight_ref.1), custom_call_target="tpu_custom_call" | custom-call | tf_op jit(solution)/shard_map/pallas_call | solution.py:303
  32.0 1.4 %reshape.11 = bf16[1,16384]{1,0:T(2,128)(2,1)} reshape(bf16[4,32,128]{2,1,0:T(8,128)(2,1)} %shard_map.55) | data formatting | bytes 65536 | tf_op jit(solution)/shard_map/reshape | solution.py:340

commit v5 on v4

--- a/solution.py
+++ b/solution.py
@@ -156,14 +156,17 @@
     lane = lax.broadcasted_iota(jnp.int32, (16, LANES), 1)
     units = per_kv // hpd
 
-    @pl.loop(0, kv_heads)
-    def _(h):
-        keys = jnp.concatenate([k_buf[...], page_hot[...]], axis=1)
-        values = jnp.concatenate([v_buf[...], jnp.ones((2 * tokens, LANES), jnp.bfloat16)], axis=1)
-        for rb in range(n // 16):
-            queries = q_aug[h, rb * 16 * per_kv:(rb + 1) * 16 * per_kv, :]
-            scores = lax.dot_general(queries, keys, (((1,), (1,)), ((), ())),
-                                     preferred_element_type=jnp.float32)
+    tiles = [(h, rb) for h in range(kv_heads) for rb in range(n // 16)]
+    keys = jnp.concatenate([k_buf[...], page_hot[...]], axis=1)
+    values = jnp.concatenate([v_buf[...], jnp.ones((2 * tokens, LANES), jnp.bfloat16)], axis=1)
+
+    def score(h, rb):
+        queries = q_aug[h, rb * 16 * per_kv:(rb + 1) * 16 * per_kv, :]
+        return lax.dot_general(queries, keys, (((1,), (1,)), ((), ())), preferred_element_type=jnp.float32)
+
+    scores = score(*tiles[0])
+    for turn, (h, rb) in enumerate(tiles):
+            upcoming = score(*tiles[turn + 1]) if turn + 1 < len(tiles) else None
             top = jnp.max(scores, axis=1, keepdims=True) * scale
             weights = jnp.exp2(scores * scale - top).astype(jnp.bfloat16)
             sums = jnp.dot(weights, values, preferred_element_type=jnp.float32)
@@ -184,16 +187,19 @@
                 packed = jnp.where(lane < 32, high.astype(jnp.float32),
                                    jnp.where(lane < 64, middle.astype(jnp.float32), low))
                 p_send[h * units + u, rows, hpd * hd:hpd * hd + LANES] = packed.astype(jnp.bfloat16)
-        for u in range(units):
-            j = h * units + u
-
-            @pl.when(j != pair)
-            def _():
-                part_copy(j).start()
-
-            @pl.when(j == pair)
-            def _():
-                p_recv[pair] = p_send[j]
+            scores = upcoming
+            if rb + 1 < n // 16:
+                continue
+            for u in range(units):
+                j = h * units + u
+
+                @pl.when(j != pair)
+                def _(j=j):
+                    part_copy(j).start()
+
+                @pl.when(j == pair)
+                def _(j=j):
+                    p_recv[pair] = p_send[j]
 
     @pl.loop(1, n)
     def _(k):
@@ -274,7 +280,9 @@
         total = f_recv[k, 0].astype(jnp.float32)
         for j in range(1, half):
             total += f_recv[k, j].astype(jnp.float32)
-        out_ref[k] = total.astype(jnp.bfloat16)
+        for b in range(blocks):
+            place = pl.ds(pl.multiple_of(k * cols + b * LANES, LANES), LANES)
+            out_ref[0:1, place] = total[b:b + 1].astype(jnp.bfloat16)
 
     @pl.loop(0, CHUNKS)
     def _(k):
@@ -300,9 +308,9 @@
     bf16, f32 = jnp.bfloat16, jnp.float32
     dma = pltpu.SemaphoreType.DMA
     vmem = pltpu.VMEM
-    out = pl.pallas_call(
+    return pl.pallas_call(
         functools.partial(kernel, dims),
-        out_shape=jax.ShapeDtypeStruct((CHUNKS, blocks, LANES), bf16),
+        out_shape=jax.ShapeDtypeStruct((1, width), bf16),
         in_specs=[pl.BlockSpec(memory_space=pl.ANY)] * 5,
         out_specs=pl.BlockSpec(memory_space=pltpu.VMEM),
         scratch_shapes=[
@@ -337,7 +345,6 @@
         compiler_params=pltpu.CompilerParams(
             collective_id=0, has_side_effects=True, vmem_limit_bytes=56 * 1024 * 1024),
     )(queries, page_ids, key_pages.reshape(tokens, hd), value_pages.reshape(tokens, hd), out_weight)
-    return out.reshape(1, width)
 
 
 def solution(mesh):

time: 33.6 us -> 33.2 us (0.988)
  Pallas kernels: 32 us -> 31.5 us
    unnamed x0 -> x1, local copies, waits for them, and re-layouts: none -> 1.54 us
    reshape x1 -> x0, local copies, waits for them, and re-layouts: 1.4 us -> none  [local(): return out.reshape(1, width)]
    pallas_call x1, Pallas kernels: 32 us -> 31.5 us  [local(): pl.pallas_call(functools.partial(kernel, dims), out_shape=jax.ShapeDtypeS...]
where the time goes in v5:
time: 33.2 us; the launch traced here: 33 us
  Pallas kernels  31.5 us (95%)
  local copies, waits for them, and re-layouts  1.54 us (5%)
    pallas_call x1, Pallas kernels, local(): pl.pallas_call(functools.partial(kernel, dims), out_shape=jax.ShapeDtypeS...  31.5 us
    unnamed x1, local copies, waits for them, and re-layouts  1.54 us

profile of v5, /device:TPU:0, one launch (start us, length us, event | category | flops | bytes accessed | tf_op | source)
XLA Modules:
  0.0 33.0 jit_solution(3142615776701045546)
XLA Ops:
  0.0 31.5 %shard_map.55 = bf16[1,16384]{1,0:T(2,128)(2,1)} custom-call(bf16[1,8192]{1,0:T(2,128)(2,1)} %q_ref.1, s32[1,4,32]{2,1,0:T(4,128)} %ids_ref.1, bf16[1024,128]{1,0:T(8,128)(2,1)} %bitcast.2, bf16[1024,128]{1,0:T(8,128)(2,1)} %bitcast.3, bf16[512,16384]{1,0:T(8,128)(2,1)} %weight_ref.1), custom_call_target="tpu_custom_call" | custom-call | tf_op jit(solution)/shard_map/pallas_call | solution.py:311
  31.5 1.5 %copy.7 = bf16[1,16384]{1,0:T(2,128)(2,1)} copy(bf16[1,16384]{1,0:T(2,128)(2,1)} %shard_map.55) | data formatting | bytes 65536
